TPU v7x, 768 devices: a whole 4x8x12 slice. The times are simulated.
768 devices in a mesh: ctx: 24 (over z, core), dp: 32 (over y, x).
Axes of the slice: x: 4, y: 8, z: 12, core: 2. Of those that a mesh axis runs over, the one named last changes fastest.
Arguments:
- query_proj: bfloat16 [98304, 32, 128], P(('dp', 'ctx')), parts along dimension 0, may hold values from -60 to 60
- key_proj: bfloat16 [98304, 4, 128], P(('dp', 'ctx')), parts along dimension 0, may hold values from -40 to 40
- value_projection: bfloat16 [98304, 4, 128], P(('dp', 'ctx')), parts along dimension 0, may hold values from -6 to 6
- lengths: int32 [1536], P('dp'), parts along dimension 0, may hold values from 1 to 384, 3072 in all
Outputs:
- attended: bfloat16 [98304, 32, 128], P(('dp', 'ctx')), parts along dimension 0
- log_sum: float32 [32, 98304], P(None, ('dp', 'ctx')), parts along dimension 1
There are 32 independent parts, one for each index of `dp`. A program takes and returns all parts, laid end to end along the dimension named above; each array names one. Nothing has to cross between parts.
Inputs may be any that keep to these rules, and one draw needn't show every extreme that they name: The lengths sum to 3072; the longest document has exactly 384 tokens.
All inputs are finite; a program needn't handle non-finite values.
Results may differ from a plain program's by a relative error of at most 0.0028.
Values may be sent and summed in bfloat16 or wider, within the bound.
No kernel may reach another device: no remote copies, remote signals or barrier semaphores. Data moves between devices by JAX's collectives and lax.ppermute only.
A program may use at most 32 MiB of HBM per device.

v0:
```python
import functools
import math

import jax
import jax.numpy as jnp
from jax import lax
from jax.experimental import pallas as pl
from jax.experimental.pallas import tpu as pltpu
from jax.sharding import PartitionSpec as P

hidden = -1e30
step_rows = 32


def lay_out_kernel(key_ref, value_ref, pair_ref, rows_ref):
    tokens, heads, _ = key_ref.shape
    for place, ref in enumerate((key_ref, value_ref)):
        rows_ref[...] = ref[...].astype(jnp.float32).reshape(rows_ref.shape)
        for head in range(heads):
            one = rows_ref[pl.ds(head, tokens, stride=heads), :]
            pair_ref[place * heads + head] = one.astype(jnp.bfloat16)


def lay_out(keys, values):
    tokens, heads, size = keys.shape
    return pl.pallas_call(
        lay_out_kernel,
        out_shape=jax.ShapeDtypeStruct((2 * heads, tokens, size), jnp.bfloat16),
        in_specs=[pl.BlockSpec(memory_space=pltpu.VMEM)] * 2,
        out_specs=pl.BlockSpec(memory_space=pltpu.VMEM),
        scratch_shapes=[pltpu.VMEM((tokens * heads, size), jnp.float32)],
        name="lay_out",
    )(keys, values)


def attend_kernel(
    lengths_ref,
    query_ref,
    own_ref,
    extra_ref,
    before_ref,
    out_ref,
    log_ref,
    key_ref,
    value_ref,
    bias_ref,
    top_ref,
    sum_ref,
):
    tokens, query_heads, size = query_ref.shape
    kv_heads = own_ref.shape[0] // 2
    group = query_heads // kv_heads
    scale = 1.0 / math.sqrt(size)
    shard = lax.axis_index("ctx")
    second = lax.rem(shard, 2) == 1
    base = shard * tokens

    lane = lax.broadcasted_iota(jnp.int32, (tokens, tokens), 1)
    row = lax.broadcasted_iota(jnp.int32, (tokens, tokens), 0)
    position = base + lane[:8]
    end = jnp.int32(0)
    start = jnp.int32(0)
    rows_of_first = jnp.int32(tokens)
    document = jnp.zeros((8, tokens), jnp.int32)
    for index in range(lengths_ref.shape[0]):
        end = end + lengths_ref[index]
        document = document + (end <= position).astype(jnp.int32)
        start = jnp.where(end <= base, end, start)
        inside = jnp.where(end > base, end - base, tokens)
        rows_of_first = jnp.minimum(rows_of_first, inside)
    reach = base - start
    remote_blocks = (reach + tokens - 1) // tokens

    by_key = jnp.broadcast_to(document[:1].astype(jnp.float32), (tokens, tokens))
    by_row = by_key.T
    own_bias = jnp.where((by_key == by_row) & (lane <= row), 0.0, hidden)
    bias_ref[3] = jnp.broadcast_to(own_bias[:, None, :], (tokens, group, tokens))
    for block in range(3):
        first_key = base - (3 - block) * tokens
        visible = (first_key + lane >= start) & (row < rows_of_first)
        bias = jnp.where(visible, 0.0, hidden)
        bias_ref[block] = jnp.broadcast_to(bias[:, None, :], (tokens, group, tokens))

    def place(block, pair, at):
        rows = slice(block * tokens, (block + 1) * tokens)
        for head in range(kv_heads):
            key_ref[head, rows, :] = pair[at + head]
            value_ref[head, rows, :size] = pair[at + kv_heads + head]

    for head in range(kv_heads):
        value_ref[head, :, size:] = jnp.ones((4 * tokens, size), jnp.bfloat16)
    place(3, own_ref, 0)

    @pl.when(second)
    def _():
        place(0, before_ref, 0)
        place(1, before_ref, 2 * kv_heads)
        place(2, extra_ref, 0)

    @pl.when(jnp.logical_not(second))
    def _():
        place(0, extra_ref, 0)
        place(1, before_ref, 0)
        place(2, before_ref, 2 * kv_heads)

    top_ref[...] = jnp.zeros_like(top_ref)
    sum_ref[...] = jnp.zeros_like(sum_ref)

    def attend_rows(first_row, blocks):
        low = 4 - blocks
        rows = pl.ds(first_row, step_rows)
        queries = query_ref[rows].astype(jnp.float32)
        hot = lax.broadcasted_iota(jnp.int32, (step_rows, group, tokens), 2) == (
            first_row + lax.broadcasted_iota(jnp.int32, (step_rows, group, tokens), 0)
        )
        results = []
        for head in range(kv_heads):
            lanes = slice(head * group, (head + 1) * group)
            one = queries[:, lanes, :].reshape(step_rows * group, size).astype(jnp.bfloat16)
            scores = lax.dot_general(
                one,
                key_ref[head, low * tokens :, :],
                (((1,), (1,)), ((), ())),
                preferred_element_type=jnp.float32,
            )
            parts = []
            for block in range(blocks):
                part = scores[:, block * tokens : (block + 1) * tokens]
                bias = bias_ref[low + block, rows]
                parts.append(part + bias.reshape(step_rows * group, tokens))
            most = functools.reduce(jnp.maximum, parts)
            top = jnp.max(most, axis=1, keepdims=True)
            weights = [jnp.exp((part - top) * scale).astype(jnp.bfloat16) for part in parts]
            total = jnp.dot(
                jnp.concatenate(weights, axis=1),
                value_ref[head, low * tokens :, :],
                preferred_element_type=jnp.float32,
            )
            row_sum = total[:, size:]
            result = total[:, :size] / row_sum
            results.append(result.reshape(step_rows, group, size))
            wide_top = jnp.broadcast_to(top, (step_rows * group, tokens))
            wide_top = wide_top.reshape(step_rows, group, tokens)
            wide_sum = row_sum.reshape(step_rows, group, tokens)
            top_ref[lanes, :] += jnp.sum(jnp.where(hot, wide_top, 0.0), axis=0)
            sum_ref[lanes, :] += jnp.sum(jnp.where(hot, wide_sum, 0.0), axis=0)
        out_ref[rows] = jnp.concatenate(results, axis=1).astype(jnp.bfloat16)

    @pl.loop(0, tokens // step_rows)
    def _(step):
        first_row = pl.multiple_of(step * step_rows, step_rows)
        needed = jnp.where(first_row < rows_of_first, remote_blocks, 0)
        for blocks in range(4):

            @pl.when(needed == blocks)
            def _():
                attend_rows(first_row, blocks + 1)

    log_ref[...] = top_ref[...] * scale + jnp.log(sum_ref[...])


def attend(lengths, queries, own, extra, before):
    tokens, query_heads, size = queries.shape
    kv_heads = own.shape[0] // 2
    group = query_heads // kv_heads
    vmem = pl.BlockSpec(memory_space=pltpu.VMEM)
    return pl.pallas_call(
        attend_kernel,
        out_shape=(
            jax.ShapeDtypeStruct((tokens, query_heads, size), jnp.bfloat16),
            jax.ShapeDtypeStruct((query_heads, tokens), jnp.float32),
        ),
        in_specs=[pl.BlockSpec(memory_space=pltpu.SMEM), vmem, vmem, vmem, vmem],
        out_specs=(vmem, vmem),
        scratch_shapes=[
            pltpu.VMEM((kv_heads, 4 * tokens, size), jnp.bfloat16),
            pltpu.VMEM((kv_heads, 4 * tokens, 2 * size), jnp.bfloat16),
            pltpu.VMEM((4, tokens, group, tokens), jnp.float32),
            pltpu.VMEM((query_heads, tokens), jnp.float32),
            pltpu.VMEM((query_heads, tokens), jnp.float32),
        ],
        compiler_params=pltpu.CompilerParams(vmem_limit_bytes=32 * 1024 * 1024),
        name="attend",
    )(lengths, queries, own, extra, before)


def per_device(query_proj, key_proj, value_projection, lengths):
    size = lax.axis_size("ctx")
    own = lay_out(key_proj, value_projection)
    by_two = [(i, i + 2) for i in range(size - 2)]
    pairs_of_chip = [[i, i + 1] for i in range(0, size, 2)]
    uneven = [(i, i + 1) for i in range(0, size, 2)] + [(i, i + 3) for i in range(1, size - 3, 2)]
    behind = lax.ppermute(own, "ctx", by_two)
    extra = lax.ppermute(own, "ctx", uneven)
    before = lax.all_gather(behind, "ctx", axis_index_groups=pairs_of_chip, axis=0, tiled=True)
    return attend(lengths, query_proj, own, extra, before)


def solution(mesh):
    return jax.shard_map(
        per_device,
        mesh=mesh,
        in_specs=(
            P(("dp", "ctx"), None, None),
            P(("dp", "ctx"), None, None),
            P(("dp", "ctx"), None, None),
            P("dp"),
        ),
        out_specs=(P(("dp", "ctx"), None, None), P(None, ("dp", "ctx"))),
        check_vma=False,
    )
```

profile of v0, /device:TPU:65, one launch (start us, length us, event | category | flops | bytes accessed | tf_op | source)
XLA Modules:
  0.0 29.2 jit_solution(7540573045121955557)
XLA Ops:
  0.6 0.0 copy-start
  0.6 1.9 %lay_out.1.own_ref = bf16[8,128,128]{2,1,0:T(8,128)(2,1)} custom-call(bf16[128,4,128]{2,1,0:T(4,128)(2,1)} %key_ref.1, bf16[128,4,128]{2,1,0:T(4,128)(2,1)} %value_ref.1), custom_call_target="tpu_custom_call" | custom-call | tf_op jit(solution)/shard_map/lay_out/pallas_call | solution.py:26
  2.5 0.0 copy-start.1
  2.5 4.1 %collective-permute-start.1 = (bf16[8,128,128]{2,1,0:T(8,128)(2,1)}, bf16[8,128,128]{2,1,0:T(8,128)(2,1)S(1)}, u32[]{:S(2)}, u32[]{:S(2)}) collective-permute-start(bf16[8,128,128]{2,1,0:T(8,128)(2,1)} %lay_out.1.own_ref), channel_id=1, source_target_pairs={{0,64},{32,96},{64,128},{96,160},{128,192},{160,224},{192,256},{22... | collective-permute-start | bytes 786440 | tf_op jit(solution)/shard_map/ppermute | solution.py:193
  6.6 7.9 %collective-permute-start = (bf16[8,128,128]{2,1,0:T(8,128)(2,1)}, bf16[8,128,128]{2,1,0:T(8,128)(2,1)S(1)}, u32[]{:S(2)}, u32[]{:S(2)}) collective-permute-start(bf16[8,128,128]{2,1,0:T(8,128)(2,1)} %lay_out.1.own_ref), channel_id=1, source_target_pairs={{0,32},{64,96},{128,160},{192,224},{256,288},{320,352},{384,416},{... | collective-permute-start | bytes 786440 | tf_op jit(solution)/shard_map/ppermute | solution.py:194
  14.5 0.0 collective-permute-done.1
  14.5 7.4 %all_gather.3.before_ref = bf16[16,128,128]{2,1,0:T(8,128)(2,1)S(1)} all-gather(bf16[8,128,128]{2,1,0:T(8,128)(2,1)S(1)} %collective-permute-done.1), channel_id=1, replica_groups={{0,32},{64,96},{128,160},{192,224},{256,288},{320,352},{384,416},{448,4..., dimensions={0}, use_global_device_ids=true | all-gather | bytes 786432 | tf_op jit(solution)/shard_map/all_gather | solution.py:195
  21.9 0.0 collective-permute-done.extra_ref
  21.9 0.0 copy-done
  21.9 0.0 copy-done.1
  21.9 0.0 copy-start.2
  21.9 0.7 %copy-done.2 = s32[48]{0:T(128)S(1)} copy-done((s32[48]{0:T(128)S(1)}, s32[48]{0:T(128)}, u32[]{:S(2)}) %copy-start.2) | copy-done | bytes 216
  22.6 6.6 %attend.1 = (bf16[128,32,128]{2,1,0:T(8,128)(2,1)}, f32[32,128]{1,0:T(8,128)}) custom-call(s32[48]{0:T(128)S(1)} %copy-done.2, bf16[128,32,128]{2,1,0:T(8,128)(2,1)S(1)} %copy-done, bf16[8,128,128]{2,1,0:T(8,128)(2,1)S(1)} %copy-done.1, bf16[8,128,128]{2,1,0:T(8,128)(2,1)S(1)} %collective-permute-done.extra_ref, bf16[16,128,128]{2,1,0:T(8,128)(2,1)S(1)} %all_gather.3.before_ref), custom_call_target="tpu_custom_call" | custom-call | tf_op jit(solution)/shard_map/attend/pallas_call | solution.py:167
Async XLA Ops:
  0.6 21.3 %copy-start = (bf16[128,32,128]{2,1,0:T(8,128)(2,1)S(1)}, bf16[128,32,128]{2,1,0:T(8,128)(2,1)}, u32[]{:S(2)}) copy-start(bf16[128,32,128]{2,1,0:T(8,128)(2,1)} %query_ref.1) | copy-start | bytes 3145732
  2.5 19.4 %copy-start.1 = (bf16[8,128,128]{2,1,0:T(8,128)(2,1)S(1)}, bf16[8,128,128]{2,1,0:T(8,128)(2,1)}, u32[]{:S(2)}) copy-start(bf16[8,128,128]{2,1,0:T(8,128)(2,1)} %lay_out.1.own_ref) | copy-start | bytes 786436
  2.5 12.0 %collective-permute-start.1 = (bf16[8,128,128]{2,1,0:T(8,128)(2,1)}, bf16[8,128,128]{2,1,0:T(8,128)(2,1)S(1)}, u32[]{:S(2)}, u32[]{:S(2)}) collective-permute-start(bf16[8,128,128]{2,1,0:T(8,128)(2,1)} %lay_out.1.own_ref), channel_id=1, source_target_pairs={{0,64},{32,96},{64,128},{96,160},{128,192},{160,224},{192,256},{22... | collective-permute-start | bytes 786440 | tf_op jit(solution)/shard_map/ppermute | solution.py:193
  6.6 15.3 %collective-permute-start = (bf16[8,128,128]{2,1,0:T(8,128)(2,1)}, bf16[8,128,128]{2,1,0:T(8,128)(2,1)S(1)}, u32[]{:S(2)}, u32[]{:S(2)}) collective-permute-start(bf16[8,128,128]{2,1,0:T(8,128)(2,1)} %lay_out.1.own_ref), channel_id=1, source_target_pairs={{0,32},{64,96},{128,160},{192,224},{256,288},{320,352},{384,416},{... | collective-permute-start | bytes 786440 | tf_op jit(solution)/shard_map/ppermute | solution.py:194
  21.9 0.7 %copy-start.2 = (s32[48]{0:T(128)S(1)}, s32[48]{0:T(128)}, u32[]{:S(2)}) copy-start(s32[48]{0:T(128)} %lengths_ref.1) | copy-start | bytes 580
where the time goes:
time: 29.3 us; the launch traced here: 29.2 us
  starting transfers between devices  12 us (41%)
  Pallas kernels  8.45 us (29%)
  blocking collectives  7.39 us (25%)
  between operations  0.67 us (2%)
  local copies, waits for them, and re-layouts  0.66 us (2%)
    ppermute x1, starting transfers between devices, per_device(): extra = lax.ppermute(own, 'ctx', uneven)  7.86 us
    all_gather x1, blocking collectives, per_device(): lax.all_gather(behind, 'ctx', axis_index_groups=pairs_of_chip, axis=0, ti...  7.39 us
    pallas_call x1, Pallas kernels, attend(): pl.pallas_call(attend_kernel, out_shape=(jax.ShapeDtypeStruct((tokens, qu...  6.59 us
    ppermute x1, starting transfers between devices, per_device(): behind = lax.ppermute(own, 'ctx', by_two)  4.12 us
    pallas_call x1, Pallas kernels, lay_out(): pl.pallas_call(lay_out_kernel, out_shape=jax.ShapeDtypeStruct((2 * heads,...  1.86 us
    unnamed x6, local copies, waits for them, and re-layouts  0.66 us
  transfers between devices with their start and end apart: 2, of which 0 were waited for; matrix products, arithmetic and copies ran while one was open for 0% of the time, Pallas kernels for 0%

commit v1 on v0

v1 whole, which is shorter than its diff:
```python
import functools
import math

import jax
import jax.numpy as jnp
from jax import lax
from jax.experimental import pallas as pl
from jax.experimental.pallas import tpu as pltpu
from jax.sharding import PartitionSpec as P

hidden = -1e30
half_rows = 64
chunk_rows = 16
pack_exponent = math.log2(math.e)


def prepare_kernel(
    all_lengths_ref, query_ref, grouped_ref, bias_ref, blocks_ref, lengths_ref, rows_ref, known, came
):
    tokens, query_heads, size = query_ref.shape
    kv_heads = grouped_ref.shape[0]
    group = query_heads // kv_heads
    part = tokens // 4
    lengths_copy = pltpu.make_async_copy(all_lengths_ref, lengths_ref, known)
    lengths_copy.start()
    copies = [
        pltpu.make_async_copy(
            query_ref.at[pl.ds(first, part)], rows_ref.at[pl.ds(first, part)], came.at[first // part]
        )
        for first in range(0, tokens, part)
    ]
    for copy in copies:
        copy.start()
    base = lax.axis_index("ctx") * tokens
    lane = lax.broadcasted_iota(jnp.int32, (tokens, tokens), 1)
    row = lax.broadcasted_iota(jnp.int32, (tokens, tokens), 0)
    position = base + lane[:8]
    end = jnp.int32(0)
    start = jnp.int32(0)
    rows_of_first = jnp.int32(tokens)
    document = jnp.zeros((8, tokens), jnp.int32)
    lengths_copy.wait()
    for index in range(lengths_ref.shape[0]):
        end = end + lengths_ref[index]
        document = document + (end <= position).astype(jnp.int32)
        start = jnp.where(end <= base, end, start)
        inside = jnp.where(end > base, end - base, tokens)
        rows_of_first = jnp.minimum(rows_of_first, inside)
    blocks_ref[...] = jnp.full(blocks_ref.shape, (base - start + tokens - 1) // tokens, jnp.int32)
    by_key = jnp.broadcast_to(document[:1].astype(jnp.float32), (tokens, tokens))
    by_row = by_key.T
    own_bias = jnp.where((by_key == by_row) & (lane <= row), 0.0, hidden)
    bias_ref[3] = jnp.broadcast_to(own_bias[:, None, :], (tokens, group, tokens))
    for block in range(3):
        first_key = base - (3 - block) * tokens
        visible = (first_key + lane >= start) & (row < rows_of_first)
        bias = jnp.where(visible, 0.0, hidden)
        bias_ref[block] = jnp.broadcast_to(bias[:, None, :], (tokens, group, tokens))
    for copy, first in zip(copies, range(0, tokens, part)):
        copy.wait()
        queries = rows_ref[first : first + part].astype(jnp.float32)
        for head in range(kv_heads):
            one = queries[:, head * group : (head + 1) * group, :].reshape(part * group, size)
            grouped_ref[head, first * group : (first + part) * group] = one.astype(jnp.bfloat16)


def prepare(lengths, queries, kv_heads):
    tokens, query_heads, size = queries.shape
    group = query_heads // kv_heads
    vmem = pl.BlockSpec(memory_space=pltpu.VMEM)
    return pl.pallas_call(
        prepare_kernel,
        out_shape=(
            jax.ShapeDtypeStruct((kv_heads, tokens * group, size), jnp.bfloat16),
            jax.ShapeDtypeStruct((4, tokens, group, tokens), jnp.float32),
            jax.ShapeDtypeStruct((8, 128), jnp.int32),
        ),
        in_specs=[pl.BlockSpec(memory_space=pltpu.HBM)] * 2,
        out_specs=(vmem, vmem, vmem),
        scratch_shapes=[
            pltpu.SMEM(lengths.shape, jnp.int32),
            pltpu.VMEM(queries.shape, jnp.bfloat16),
            pltpu.SemaphoreType.DMA,
            pltpu.SemaphoreType.DMA((4,)),
        ],
        compiler_params=pltpu.CompilerParams(vmem_limit_bytes=16 * 1024 * 1024),
        name="prepare",
    )(
        pltpu.with_memory_space_constraint(lengths, pltpu.HBM),
        pltpu.with_memory_space_constraint(queries, pltpu.HBM),
    )


def attend_kernel(
    blocks_ref,
    query_ref,
    bias_ref,
    own_ref,
    second_far_ref,
    first_near_ref,
    first_far_ref,
    second_near_ref,
    second_mid_ref,
    first_mid_ref,
    out_ref,
    log_ref,
    key_ref,
    value_ref,
    result_ref,
    rows_ref,
    logs_ref,
    totals_ref,
    sent,
    log_sent,
):
    kv_heads, stacked, size = query_ref.shape
    tokens = own_ref.shape[1]
    group = stacked // tokens
    scale = 1.0 / math.sqrt(size)
    shard = lax.axis_index("ctx")
    second = lax.rem(shard, 2) == 1
    remote_blocks = blocks_ref[0, 0]

    def place(block, pair_ref):
        rows = slice(block * tokens, (block + 1) * tokens)
        for head in range(kv_heads):
            key_ref[head, rows, :] = pair_ref[head]
            value_ref[head, rows, :size] = pair_ref[kv_heads + head]

    for head in range(kv_heads):
        value_ref[head, :, size:] = jnp.ones((4 * tokens, size), jnp.bfloat16)
    place(3, own_ref)

    @pl.when(second)
    def _():
        place(0, second_far_ref)
        place(1, second_mid_ref)
        place(2, second_near_ref)

    @pl.when(jnp.logical_not(second))
    def _():
        place(0, first_far_ref)
        place(1, first_mid_ref)
        place(2, first_near_ref)

    lane = lax.broadcasted_iota(jnp.int32, (group, tokens), 1)
    chunk = chunk_rows * group
    pairs, halves = kv_heads // 2, tokens // half_rows
    work = [
        (pair, 2 * pair + head, first)
        for pair in range(pairs)
        for head in range(2)
        for first in range(0, half_rows, chunk_rows)
    ]

    def copy_out(pair, half):
        rows = pl.ds(half * half_rows, half_rows)
        heads = pl.ds(2 * pair * group, 2 * group)
        return pltpu.make_async_copy(
            rows_ref.at[pair, half], out_ref.at[rows, heads], sent.at[pair, half]
        )

    def attend_half(half, blocks):
        low = 4 - blocks
        row_of_half = pl.multiple_of(half * half_rows, half_rows)
        logs = {
            head: tuple(
                totals_ref[part, head * group : (head + 1) * group, :] for part in range(2)
            )
            for head in range(kv_heads)
        }

        def score(item):
            _, head, first = item
            return lax.dot_general(
                query_ref[head, pl.ds((row_of_half + first) * group, chunk), :],
                key_ref[head, low * tokens :, :],
                (((1,), (1,)), ((), ())),
                preferred_element_type=jnp.float32,
            )

        def weigh(item, scores):
            _, _, first = item
            parts = []
            for block in range(blocks):
                part = scores[:, block * tokens : (block + 1) * tokens]
                bias = bias_ref[low + block, pl.ds(row_of_half + first, chunk_rows)]
                parts.append(part + bias.reshape(chunk, tokens))
            top = jnp.max(functools.reduce(jnp.maximum, parts), axis=1, keepdims=True)
            weights = [
                jnp.exp2((part - top) * (scale * pack_exponent)).astype(jnp.bfloat16)
                for part in parts
            ]
            return top, jnp.concatenate(weights, axis=1)

        def gather(item, top, weights):
            pair, head, first = item
            total = jnp.dot(
                weights, value_ref[head, low * tokens :, :], preferred_element_type=jnp.float32
            )
            row_sum = total[:, size:]
            share = pl.reciprocal(row_sum, approx=True)
            share = share * (2.0 - row_sum * share)
            result = total[:, :size] * share
            place_of_head = (head % 2) * group
            result_ref[
                pair, first : first + chunk_rows, place_of_head : place_of_head + group
            ] = result.reshape(chunk_rows, group, size)
            wide_top = jnp.broadcast_to(top, (chunk, tokens)).reshape(chunk_rows, group, tokens)
            wide_sum = row_sum.reshape(chunk_rows, group, tokens)
            tops, sums = logs[head]
            for row in range(chunk_rows):
                hot = lane == row_of_half + first + row
                tops = jnp.where(hot, wide_top[row], tops)
                sums = jnp.where(hot, wide_sum[row], sums)
            logs[head] = (tops, sums)
            if head % 2 == 1 and first + chunk_rows == half_rows:
                rows_ref[pair, half] = result_ref[pair].astype(jnp.bfloat16)
                copy_out(pair, half).start()

        scored, weighed = {}, {}
        count = len(work)
        for step in range(count + 2):
            if step < count:
                scored[step] = score(work[step])
            if 0 <= step - 1 < count:
                weighed[step - 1] = weigh(work[step - 1], scored.pop(step - 1))
            if 0 <= step - 2 < count:
                gather(work[step - 2], *weighed.pop(step - 2))
        for head in range(kv_heads):
            for part in range(2):
                totals_ref[part, head * group : (head + 1) * group, :] = logs[head][part]

    totals_ref[...] = jnp.ones_like(totals_ref)

    @pl.loop(0, halves)
    def _(half):
        @pl.when(remote_blocks < 2)
        def _():
            attend_half(half, 2)

        @pl.when(remote_blocks >= 2)
        def _():
            attend_half(half, 4)

    logs_ref[...] = totals_ref[0] * scale + jnp.log(totals_ref[1])
    log_copy = pltpu.make_async_copy(logs_ref, log_ref, log_sent)
    log_copy.start()
    for pair in range(pairs):
        for half in range(halves):
            copy_out(pair, half).wait()
    log_copy.wait()


def attend(prepared, own, earlier):
    grouped, bias, remote_blocks = prepared
    kv_heads, tokens, size = own.shape[0] // 2, own.shape[1], own.shape[2]
    group = grouped.shape[1] // tokens
    query_heads = kv_heads * group
    pairs, halves = kv_heads // 2, tokens // half_rows
    vmem = pl.BlockSpec(memory_space=pltpu.VMEM)
    return pl.pallas_call(
        attend_kernel,
        out_shape=(
            jax.ShapeDtypeStruct((tokens, query_heads, size), jnp.bfloat16),
            jax.ShapeDtypeStruct((query_heads, tokens), jnp.float32),
        ),
        in_specs=[vmem] * 10,
        out_specs=(pl.BlockSpec(memory_space=pl.ANY), pl.BlockSpec(memory_space=pl.ANY)),
        scratch_shapes=[
            pltpu.VMEM((kv_heads, 4 * tokens, size), jnp.bfloat16),
            pltpu.VMEM((kv_heads, 4 * tokens, 2 * size), jnp.bfloat16),
            pltpu.VMEM((pairs, half_rows, 2 * group, size), jnp.float32),
            pltpu.VMEM((pairs, halves, half_rows, 2 * group, size), jnp.bfloat16),
            pltpu.VMEM((query_heads, tokens), jnp.float32),
            pltpu.VMEM((2, query_heads, tokens), jnp.float32),
            pltpu.SemaphoreType.DMA((pairs, halves)),
            pltpu.SemaphoreType.DMA,
        ],
        compiler_params=pltpu.CompilerParams(vmem_limit_bytes=24 * 1024 * 1024),
        name="attend",
    )(remote_blocks, grouped, bias, own, *earlier)


def per_device(query_proj, key_proj, value_projection, lengths):
    size = lax.axis_size("ctx")
    tokens, kv_heads, head_size = key_proj.shape
    own = jnp.stack((key_proj, value_projection)).transpose(0, 2, 1, 3)
    own = own.reshape(2 * kv_heads, tokens, head_size)
    firsts, seconds = range(0, size, 2), range(1, size, 2)

    def move(array, starts, by):
        return lax.ppermute(array, "ctx", [(i, i + by) for i in starts if 0 <= i + by < size])

    second_mid = move(own, seconds, 2)
    first_mid = move(own, firsts, 2)
    second_near = move(own, firsts, 1)
    prepared = prepare(lengths, query_proj, kv_heads)
    passed_second, _ = lax.optimization_barrier((second_mid, prepared[2][:1, :1] * 3))
    passed_first, _ = lax.optimization_barrier((first_mid, prepared[2]))
    first_far = move(passed_second, seconds[1:], 1)
    first_near = move(passed_second, seconds[1:], -1)
    second_far = move(passed_first, firsts[1:], 1)
    earlier = (second_far, first_near, first_far, second_near, second_mid, first_mid)
    return attend(prepared, own, earlier)


def solution(mesh):
    return jax.shard_map(
        per_device,
        mesh=mesh,
        in_specs=(
            P(("dp", "ctx"), None, None),
            P(("dp", "ctx"), None, None),
            P(("dp", "ctx"), None, None),
            P("dp"),
        ),
        out_specs=(P(("dp", "ctx"), None, None), P(None, ("dp", "ctx"))),
        check_vma=False,
    )
```

time: 29.3 us -> 24.7 us (0.84)
  the two profiles are of different devices: /device:TPU:65 before, /device:TPU:243 now
where the time goes in v1:
time: 24.7 us; the launch traced here: 24.5 us
  starting transfers between devices  14 us (57%)
  Pallas kernels  5.61 us (23%)
  waiting for transfers between devices  2.91 us (12%)
  other arithmetic  1.16 us (5%)
  between operations  0.71 us (3%)
    ppermute x6, starting transfers between devices, move(): lax.ppermute(array, 'ctx', [(i, i + by) for i in starts if 0 <= i + by <...  14 us
    pallas_call x1, Pallas kernels, attend(): pl.pallas_call(attend_kernel, out_shape=(jax.ShapeDtypeStruct((tokens, qu...  4.18 us
    ppermute x6, waiting for transfers between devices, move(): lax.ppermute(array, 'ctx', [(i, i + by) for i in starts if 0 <= i + by <...  2.91 us
    pallas_call x1, Pallas kernels, prepare(): pl.pallas_call(prepare_kernel, out_shape=(jax.ShapeDtypeStruct((kv_heads,...  1.44 us
    transpose x1, other arithmetic, per_device(): own = jnp.stack((key_proj, value_projection)).transpose(0, 2, 1, 3)  1.16 us
  transfers between devices with their start and end apart: 6, of which 3 were waited for; matrix products, arithmetic and copies ran while one was open for 0% of the time, Pallas kernels for 6%

profile of v1, /device:TPU:243, one launch (start us, length us, event | category | flops | bytes accessed | tf_op | source)
XLA Modules:
  0.0 24.5 jit_solution(9746687606565786772)
XLA Ops:
  0.6 1.2 %maximum_bitcast_fusion = bf16[2,4,128,128]{3,1,2,0:T(4,128)(2,1)S(1)} fusion(bf16[1,128,4,128]{3,2,1,0:T(4,128)(2,1)} %bitcast.9, bf16[1,128,4,128]{3,2,1,0:T(4,128)(2,1)} %bitcast.10), kind=kLoop, calls=%fused_computation | loop fusion | flops 131072 | bytes 524288 | tf_op jit(solution)/shard_map/transpose | solution.py:288
  1.8 5.2 %collective-permute-start.2 = (bf16[8,128,128]{2,1,0:T(8,128)(2,1)S(1)}, bf16[8,128,128]{2,1,0:T(8,128)(2,1)S(1)}, u32[]{:S(2)}, u32[]{:S(2)}) collective-permute-start(bf16[8,128,128]{2,1,0:T(8,128)(2,1)S(1)} %bitcast.5), channel_id=1, source_target_pairs={{32,96},{96,160},{160,224},{224,288},{288,352},{352,416},{416,480}... | collective-permute-start | bytes 786440 | tf_op jit(solution)/shard_map/ppermute | solution.py:293
  7.1 0.7 %collective-permute-start = (bf16[8,128,128]{2,1,0:T(8,128)(2,1)S(1)}, bf16[8,128,128]{2,1,0:T(8,128)(2,1)S(1)}, u32[]{:S(2)}, u32[]{:S(2)}) collective-permute-start(bf16[8,128,128]{2,1,0:T(8,128)(2,1)S(1)} %bitcast.6), channel_id=1, source_target_pairs={{0,64},{64,128},{128,192},{192,256},{256,320},{320,384},{384,448},... | collective-permute-start | bytes 786440 | tf_op jit(solution)/shard_map/ppermute | solution.py:293
  7.7 1.3 %collective-permute-start.5 = (bf16[8,128,128]{2,1,0:T(8,128)(2,1)S(1)}, bf16[8,128,128]{2,1,0:T(8,128)(2,1)S(1)}, u32[]{:S(2)}, u32[]{:S(2)}) collective-permute-start(bf16[8,128,128]{2,1,0:T(8,128)(2,1)S(1)} %bitcast.7), channel_id=1, source_target_pairs={{0,32},{64,96},{128,160},{192,224},{256,288},{320,352},{384,416},{... | collective-permute-start | bytes 786440 | tf_op jit(solution)/shard_map/ppermute | solution.py:293
  9.0 1.4 %prepare.1 = (bf16[4,1024,128]{2,1,0:T(8,128)(2,1)S(1)}, f32[4,128,8,128]{3,2,1,0:T(8,128)S(1)}, s32[8,128]{1,0:T(8,128)S(1)}) custom-call(s32[48]{0:T(128)} %all_lengths_ref.1, bf16[128,32,128]{2,1,0:T(8,128)(2,1)} %query_ref.1), custom_call_target="tpu_custom_call" | custom-call | tf_op jit(solution)/shard_map/prepare/pallas_call | solution.py:71
  10.5 0.8 %collective-permute-done.2.second_mid_ref = bf16[8,128,128]{2,1,0:T(8,128)(2,1)S(1)} collective-permute-done((bf16[8,128,128]{2,1,0:T(8,128)(2,1)S(1)}, bf16[8,128,128]{2,1,0:T(8,128)(2,1)S(1)}, u32[]{:S(2)}, u32[]{:S(2)}) %collective-permute-start.2) | collective-permute-done | bytes 262176 | tf_op jit(solution)/shard_map/ppermute | solution.py:293
  11.3 4.3 %collective-permute-start.4 = (bf16[8,128,128]{2,1,0:T(8,128)(2,1)S(1)}, bf16[8,128,128]{2,1,0:T(8,128)(2,1)S(1)}, u32[]{:S(2)}, u32[]{:S(2)}) collective-permute-start(bf16[8,128,128]{2,1,0:T(8,128)(2,1)S(1)} %collective-permute-done.2.second_mid_ref), channel_id=1, source_target_pairs={{96,128},{160,192},{224,256},{288,320},{352,384},{416,448},{480,51... | collective-permute-start | bytes 786440 | tf_op jit(solution)/shard_map/ppermute | solution.py:293
  15.5 1.3 %collective-permute-start.3 = (bf16[8,128,128]{2,1,0:T(8,128)(2,1)S(1)}, bf16[8,128,128]{2,1,0:T(8,128)(2,1)S(1)}, u32[]{:S(2)}, u32[]{:S(2)}) collective-permute-start(bf16[8,128,128]{2,1,0:T(8,128)(2,1)S(1)} %collective-permute-done.2.second_mid_ref), channel_id=1, source_target_pairs={{96,64},{160,128},{224,192},{288,256},{352,320},{416,384},{480,448... | collective-permute-start | bytes 786440 | tf_op jit(solution)/shard_map/ppermute | solution.py:293
  16.9 0.0 collective-permute-done.first_mid_ref
  16.9 1.3 %collective-permute-start.1 = (bf16[8,128,128]{2,1,0:T(8,128)(2,1)S(1)}, bf16[8,128,128]{2,1,0:T(8,128)(2,1)S(1)}, u32[]{:S(2)}, u32[]{:S(2)}) collective-permute-start(bf16[8,128,128]{2,1,0:T(8,128)(2,1)S(1)} %collective-permute-done.first_mid_ref), channel_id=1, source_target_pairs={{64,96},{128,160},{192,224},{256,288},{320,352},{384,416},{448,480... | collective-permute-start | bytes 786440 | tf_op jit(solution)/shard_map/ppermute | solution.py:293
  18.2 0.0 collective-permute-done.5.second_near_ref
  18.2 0.6 %collective-permute-done.4.first_far_ref = bf16[8,128,128]{2,1,0:T(8,128)(2,1)S(1)} collective-permute-done((bf16[8,128,128]{2,1,0:T(8,128)(2,1)S(1)}, bf16[8,128,128]{2,1,0:T(8,128)(2,1)S(1)}, u32[]{:S(2)}, u32[]{:S(2)}) %collective-permute-start.4) | collective-permute-done | bytes 262176 | tf_op jit(solution)/shard_map/ppermute | solution.py:293
  18.8 0.0 collective-permute-done.3.first_near_ref
  18.8 1.5 %collective-permute-done.1.second_far_ref = bf16[8,128,128]{2,1,0:T(8,128)(2,1)S(1)} collective-permute-done((bf16[8,128,128]{2,1,0:T(8,128)(2,1)S(1)}, bf16[8,128,128]{2,1,0:T(8,128)(2,1)S(1)}, u32[]{:S(2)}, u32[]{:S(2)}) %collective-permute-start.1) | collective-permute-done | bytes 262176 | tf_op jit(solution)/shard_map/ppermute | solution.py:293
  20.3 4.2 %attend.1 = (bf16[128,32,128]{2,1,0:T(8,128)(2,1)}, f32[32,128]{1,0:T(8,128)}) custom-call(s32[8,128]{1,0:T(8,128)S(1)} %get-tuple-element.6.blocks_ref, bf16[4,1024,128]{2,1,0:T(8,128)(2,1)S(1)} %get-tuple-element.7.query_ref, f32[4,128,8,128]{3,2,1,0:T(8,128)S(1)} %get-tuple-element.8.bias_ref, bf16[8,128,128]{2,1,0:T(8,128)(2,1)S(1)} %bitcast.8, ...), custom_call_target="tpu_custom_call" | custom-call | tf_op jit(solution)/shard_map/attend/pallas_call | solution.py:262
  (1 shorter events, 0.0 us)
Async XLA Ops:
  1.8 9.4 %collective-permute-start.2 = (bf16[8,128,128]{2,1,0:T(8,128)(2,1)S(1)}, bf16[8,128,128]{2,1,0:T(8,128)(2,1)S(1)}, u32[]{:S(2)}, u32[]{:S(2)}) collective-permute-start(bf16[8,128,128]{2,1,0:T(8,128)(2,1)S(1)} %bitcast.5), channel_id=1, source_target_pairs={{32,96},{96,160},{160,224},{224,288},{288,352},{352,416},{416,480}... | collective-permute-start | bytes 786440 | tf_op jit(solution)/shard_map/ppermute | solution.py:293
  7.1 9.8 %collective-permute-start = (bf16[8,128,128]{2,1,0:T(8,128)(2,1)S(1)}, bf16[8,128,128]{2,1,0:T(8,128)(2,1)S(1)}, u32[]{:S(2)}, u32[]{:S(2)}) collective-permute-start(bf16[8,128,128]{2,1,0:T(8,128)(2,1)S(1)} %bitcast.6), channel_id=1, source_target_pairs={{0,64},{64,128},{128,192},{192,256},{256,320},{320,384},{384,448},... | collective-permute-start | bytes 786440 | tf_op jit(solution)/shard_map/ppermute | solution.py:293
  7.7 10.4 %collective-permute-start.5 = (bf16[8,128,128]{2,1,0:T(8,128)(2,1)S(1)}, bf16[8,128,128]{2,1,0:T(8,128)(2,1)S(1)}, u32[]{:S(2)}, u32[]{:S(2)}) collective-permute-start(bf16[8,128,128]{2,1,0:T(8,128)(2,1)S(1)} %bitcast.7), channel_id=1, source_target_pairs={{0,32},{64,96},{128,160},{192,224},{256,288},{320,352},{384,416},{... | collective-permute-start | bytes 786440 | tf_op jit(solution)/shard_map/ppermute | solution.py:293
  11.3 7.5 %collective-permute-start.4 = (bf16[8,128,128]{2,1,0:T(8,128)(2,1)S(1)}, bf16[8,128,128]{2,1,0:T(8,128)(2,1)S(1)}, u32[]{:S(2)}, u32[]{:S(2)}) collective-permute-start(bf16[8,128,128]{2,1,0:T(8,128)(2,1)S(1)} %collective-permute-done.2.second_mid_ref), channel_id=1, source_target_pairs={{96,128},{160,192},{224,256},{288,320},{352,384},{416,448},{480,51... | collective-permute-start | bytes 786440 | tf_op jit(solution)/shard_map/ppermute | solution.py:293
  15.5 3.3 %collective-permute-start.3 = (bf16[8,128,128]{2,1,0:T(8,128)(2,1)S(1)}, bf16[8,128,128]{2,1,0:T(8,128)(2,1)S(1)}, u32[]{:S(2)}, u32[]{:S(2)}) collective-permute-start(bf16[8,128,128]{2,1,0:T(8,128)(2,1)S(1)} %collective-permute-done.2.second_mid_ref), channel_id=1, source_target_pairs={{96,64},{160,128},{224,192},{288,256},{352,320},{416,384},{480,448... | collective-permute-start | bytes 786440 | tf_op jit(solution)/shard_map/ppermute | solution.py:293
  16.9 3.4 %collective-permute-start.1 = (bf16[8,128,128]{2,1,0:T(8,128)(2,1)S(1)}, bf16[8,128,128]{2,1,0:T(8,128)(2,1)S(1)}, u32[]{:S(2)}, u32[]{:S(2)}) collective-permute-start(bf16[8,128,128]{2,1,0:T(8,128)(2,1)S(1)} %collective-permute-done.first_mid_ref), channel_id=1, source_target_pairs={{64,96},{128,160},{192,224},{256,288},{320,352},{384,416},{448,480... | collective-permute-start | bytes 786440 | tf_op jit(solution)/shard_map/ppermute | solution.py:293

commit v2 on v1

--- a/solution.py
+++ b/solution.py
@@ -146,12 +146,6 @@
     lane = lax.broadcasted_iota(jnp.int32, (group, tokens), 1)
     chunk = chunk_rows * group
     pairs, halves = kv_heads // 2, tokens // half_rows
-    work = [
-        (pair, 2 * pair + head, first)
-        for pair in range(pairs)
-        for head in range(2)
-        for first in range(0, half_rows, chunk_rows)
-    ]
 
     def copy_out(pair, half):
         rows = pl.ds(half * half_rows, half_rows)
@@ -160,9 +154,19 @@
             rows_ref.at[pair, half], out_ref.at[rows, heads], sent.at[pair, half]
         )
 
-    def attend_half(half, blocks):
+    def attend_rows(its_halves, blocks):
         low = 4 - blocks
-        row_of_half = pl.multiple_of(half * half_rows, half_rows)
+        work = [
+            (half, pair, 2 * pair + head, first)
+            for half in its_halves
+            for pair in range(pairs)
+            for head in range(2)
+            for first in range(0, half_rows, chunk_rows)
+        ]
+
+        def start_of(half, first):
+            return half * half_rows + first
+
         logs = {
             head: tuple(
                 totals_ref[part, head * group : (head + 1) * group, :] for part in range(2)
@@ -171,20 +175,20 @@
         }
 
         def score(item):
-            _, head, first = item
+            half, _, head, first = item
             return lax.dot_general(
-                query_ref[head, pl.ds((row_of_half + first) * group, chunk), :],
+                query_ref[head, pl.ds(start_of(half, first) * group, chunk), :],
                 key_ref[head, low * tokens :, :],
                 (((1,), (1,)), ((), ())),
                 preferred_element_type=jnp.float32,
             )
 
         def weigh(item, scores):
-            _, _, first = item
+            half, _, _, first = item
             parts = []
             for block in range(blocks):
                 part = scores[:, block * tokens : (block + 1) * tokens]
-                bias = bias_ref[low + block, pl.ds(row_of_half + first, chunk_rows)]
+                bias = bias_ref[low + block, pl.ds(start_of(half, first), chunk_rows)]
                 parts.append(part + bias.reshape(chunk, tokens))
             top = jnp.max(functools.reduce(jnp.maximum, parts), axis=1, keepdims=True)
             weights = [
@@ -194,13 +198,12 @@
             return top, jnp.concatenate(weights, axis=1)
 
         def gather(item, top, weights):
-            pair, head, first = item
+            half, pair, head, first = item
             total = jnp.dot(
                 weights, value_ref[head, low * tokens :, :], preferred_element_type=jnp.float32
             )
             row_sum = total[:, size:]
             share = pl.reciprocal(row_sum, approx=True)
-            share = share * (2.0 - row_sum * share)
             result = total[:, :size] * share
             place_of_head = (head % 2) * group
             result_ref[
@@ -210,7 +213,7 @@
             wide_sum = row_sum.reshape(chunk_rows, group, tokens)
             tops, sums = logs[head]
             for row in range(chunk_rows):
-                hot = lane == row_of_half + first + row
+                hot = lane == start_of(half, first) + row
                 tops = jnp.where(hot, wide_top[row], tops)
                 sums = jnp.where(hot, wide_sum[row], sums)
             logs[head] = (tops, sums)
@@ -233,15 +236,15 @@
 
     totals_ref[...] = jnp.ones_like(totals_ref)
 
-    @pl.loop(0, halves)
-    def _(half):
-        @pl.when(remote_blocks < 2)
-        def _():
-            attend_half(half, 2)
-
-        @pl.when(remote_blocks >= 2)
-        def _():
-            attend_half(half, 4)
+    @pl.when(remote_blocks < 2)
+    def _():
+        @pl.loop(0, halves)
+        def _(half):
+            attend_rows([half], 2)
+
+    @pl.when(remote_blocks >= 2)
+    def _():
+        attend_rows(range(halves), 4)
 
     logs_ref[...] = totals_ref[0] * scale + jnp.log(totals_ref[1])
     log_copy = pltpu.make_async_copy(logs_ref, log_ref, log_sent)
@@ -296,11 +299,9 @@
     first_mid = move(own, firsts, 2)
     second_near = move(own, firsts, 1)
     prepared = prepare(lengths, query_proj, kv_heads)
-    passed_second, _ = lax.optimization_barrier((second_mid, prepared[2][:1, :1] * 3))
-    passed_first, _ = lax.optimization_barrier((first_mid, prepared[2]))
-    first_far = move(passed_second, seconds[1:], 1)
-    first_near = move(passed_second, seconds[1:], -1)
-    second_far = move(passed_first, firsts[1:], 1)
+    first_far = move(second_mid, seconds[1:], 1)
+    first_near = move(second_mid, seconds[1:], -1)
+    second_far = move(first_mid, firsts[1:], 1)
     earlier = (second_far, first_near, first_far, second_near, second_mid, first_mid)
     return attend(prepared, own, earlier)
 

time: 24.7 us -> 22.8 us (0.923)
  the two profiles are of different devices: /device:TPU:243 before, /device:TPU:65 now
where the time goes in v2:
time: 22.8 us; the launch traced here: 22.6 us
  starting transfers between devices  11.4 us (50%)
  waiting for transfers between devices  5.04 us (22%)
  Pallas kernels  4.2 us (18%)
  other arithmetic  1.16 us (5%)
  between operations  0.73 us (3%)
    ppermute x6, starting transfers between devices, move(): lax.ppermute(array, 'ctx', [(i, i + by) for i in starts if 0 <= i + by <...  11.4 us
    ppermute x6, waiting for transfers between devices, move(): lax.ppermute(array, 'ctx', [(i, i + by) for i in starts if 0 <= i + by <...  5.04 us
    pallas_call x1, Pallas kernels, attend(): pl.pallas_call(attend_kernel, out_shape=(jax.ShapeDtypeStruct((tokens, qu...  2.77 us
    pallas_call x1, Pallas kernels, prepare(): pl.pallas_call(prepare_kernel, out_shape=(jax.ShapeDtypeStruct((kv_heads,...  1.44 us
    transpose x1, other arithmetic, per_device(): own = jnp.stack((key_proj, value_projection)).transpose(0, 2, 1, 3)  1.16 us
  transfers between devices with their start and end apart: 6, of which 2 were waited for; matrix products, arithmetic and copies ran while one was open for 0% of the time, Pallas kernels for 6%

profile of v2, /device:TPU:65, one launch (start us, length us, event | category | flops | bytes accessed | tf_op | source)
XLA Modules:
  0.0 22.6 jit_solution(14969966181137427437)
XLA Ops:
  0.6 1.2 %maximum_bitcast_fusion = bf16[2,4,128,128]{3,1,2,0:T(4,128)(2,1)S(1)} fusion(bf16[1,128,4,128]{3,2,1,0:T(4,128)(2,1)} %bitcast.9, bf16[1,128,4,128]{3,2,1,0:T(4,128)(2,1)} %bitcast.10), kind=kLoop, calls=%fused_computation | loop fusion | flops 131072 | bytes 524288 | tf_op jit(solution)/shard_map/transpose | solution.py:291
  1.8 4.0 %collective-permute-start.2 = (bf16[8,128,128]{2,1,0:T(8,128)(2,1)S(1)}, bf16[8,128,128]{2,1,0:T(8,128)(2,1)S(1)}, u32[]{:S(2)}, u32[]{:S(2)}) collective-permute-start(bf16[8,128,128]{2,1,0:T(8,128)(2,1)S(1)} %bitcast.5), channel_id=1, source_target_pairs={{32,96},{96,160},{160,224},{224,288},{288,352},{352,416},{416,480}... | collective-permute-start | bytes 786440 | tf_op jit(solution)/shard_map/ppermute | solution.py:296
  5.8 0.7 %collective-permute-start = (bf16[8,128,128]{2,1,0:T(8,128)(2,1)S(1)}, bf16[8,128,128]{2,1,0:T(8,128)(2,1)S(1)}, u32[]{:S(2)}, u32[]{:S(2)}) collective-permute-start(bf16[8,128,128]{2,1,0:T(8,128)(2,1)S(1)} %bitcast.6), channel_id=1, source_target_pairs={{0,64},{64,128},{128,192},{192,256},{256,320},{320,384},{384,448},... | collective-permute-start | bytes 786440 | tf_op jit(solution)/shard_map/ppermute | solution.py:296
  6.5 1.3 %collective-permute-start.5 = (bf16[8,128,128]{2,1,0:T(8,128)(2,1)S(1)}, bf16[8,128,128]{2,1,0:T(8,128)(2,1)S(1)}, u32[]{:S(2)}, u32[]{:S(2)}) collective-permute-start(bf16[8,128,128]{2,1,0:T(8,128)(2,1)S(1)} %bitcast.7), channel_id=1, source_target_pairs={{0,32},{64,96},{128,160},{192,224},{256,288},{320,352},{384,416},{... | collective-permute-start | bytes 786440 | tf_op jit(solution)/shard_map/ppermute | solution.py:296
  7.8 2.2 %collective-permute-done.2.second_mid_ref = bf16[8,128,128]{2,1,0:T(8,128)(2,1)S(1)} collective-permute-done((bf16[8,128,128]{2,1,0:T(8,128)(2,1)S(1)}, bf16[8,128,128]{2,1,0:T(8,128)(2,1)S(1)}, u32[]{:S(2)}, u32[]{:S(2)}) %collective-permute-start.2) | collective-permute-done | bytes 262176 | tf_op jit(solution)/shard_map/ppermute | solution.py:296
  10.1 2.8 %collective-permute-start.4 = (bf16[8,128,128]{2,1,0:T(8,128)(2,1)S(1)}, bf16[8,128,128]{2,1,0:T(8,128)(2,1)S(1)}, u32[]{:S(2)}, u32[]{:S(2)}) collective-permute-start(bf16[8,128,128]{2,1,0:T(8,128)(2,1)S(1)} %collective-permute-done.2.second_mid_ref), channel_id=1, source_target_pairs={{96,128},{160,192},{224,256},{288,320},{352,384},{416,448},{480,51... | collective-permute-start | bytes 786440 | tf_op jit(solution)/shard_map/ppermute | solution.py:296
  12.9 1.3 %collective-permute-start.3 = (bf16[8,128,128]{2,1,0:T(8,128)(2,1)S(1)}, bf16[8,128,128]{2,1,0:T(8,128)(2,1)S(1)}, u32[]{:S(2)}, u32[]{:S(2)}) collective-permute-start(bf16[8,128,128]{2,1,0:T(8,128)(2,1)S(1)} %collective-permute-done.2.second_mid_ref), channel_id=1, source_target_pairs={{96,64},{160,128},{224,192},{288,256},{352,320},{416,384},{480,448... | collective-permute-start | bytes 786440 | tf_op jit(solution)/shard_map/ppermute | solution.py:296
  14.2 0.0 collective-permute-done.first_mid_ref
  14.2 1.3 %collective-permute-start.1 = (bf16[8,128,128]{2,1,0:T(8,128)(2,1)S(1)}, bf16[8,128,128]{2,1,0:T(8,128)(2,1)S(1)}, u32[]{:S(2)}, u32[]{:S(2)}) collective-permute-start(bf16[8,128,128]{2,1,0:T(8,128)(2,1)S(1)} %collective-permute-done.first_mid_ref), channel_id=1, source_target_pairs={{64,96},{128,160},{192,224},{256,288},{320,352},{384,416},{448,480... | collective-permute-start | bytes 786440 | tf_op jit(solution)/shard_map/ppermute | solution.py:296
  15.5 1.4 %prepare.1 = (bf16[4,1024,128]{2,1,0:T(8,128)(2,1)S(1)}, f32[4,128,8,128]{3,2,1,0:T(8,128)S(1)}, s32[8,128]{1,0:T(8,128)S(1)}) custom-call(s32[48]{0:T(128)} %all_lengths_ref.1, bf16[128,32,128]{2,1,0:T(8,128)(2,1)} %query_ref.1), custom_call_target="tpu_custom_call" | custom-call | tf_op jit(solution)/shard_map/prepare/pallas_call | solution.py:71
  17.0 0.0 collective-permute-done.5.second_near_ref
  17.0 0.0 collective-permute-done.4.first_far_ref
  17.0 0.0 collective-permute-done.3.first_near_ref
  17.0 2.8 %collective-permute-done.1.second_far_ref = bf16[8,128,128]{2,1,0:T(8,128)(2,1)S(1)} collective-permute-done((bf16[8,128,128]{2,1,0:T(8,128)(2,1)S(1)}, bf16[8,128,128]{2,1,0:T(8,128)(2,1)S(1)}, u32[]{:S(2)}, u32[]{:S(2)}) %collective-permute-start.1) | collective-permute-done | bytes 262176 | tf_op jit(solution)/shard_map/ppermute | solution.py:296
  19.8 2.8 %attend.1 = (bf16[128,32,128]{2,1,0:T(8,128)(2,1)}, f32[32,128]{1,0:T(8,128)}) custom-call(s32[8,128]{1,0:T(8,128)S(1)} %get-tuple-element.5.blocks_ref, bf16[4,1024,128]{2,1,0:T(8,128)(2,1)S(1)} %get-tuple-element.6.query_ref, f32[4,128,8,128]{3,2,1,0:T(8,128)S(1)} %get-tuple-element.7.bias_ref, bf16[8,128,128]{2,1,0:T(8,128)(2,1)S(1)} %bitcast.8, ...), custom_call_target="tpu_custom_call" | custom-call | tf_op jit(solution)/shard_map/attend/pallas_call | solution.py:265
  (1 shorter events, 0.0 us)
Async XLA Ops:
  1.8 8.2 %collective-permute-start.2 = (bf16[8,128,128]{2,1,0:T(8,128)(2,1)S(1)}, bf16[8,128,128]{2,1,0:T(8,128)(2,1)S(1)}, u32[]{:S(2)}, u32[]{:S(2)}) collective-permute-start(bf16[8,128,128]{2,1,0:T(8,128)(2,1)S(1)} %bitcast.5), channel_id=1, source_target_pairs={{32,96},{96,160},{160,224},{224,288},{288,352},{352,416},{416,480}... | collective-permute-start | bytes 786440 | tf_op jit(solution)/shard_map/ppermute | solution.py:296
  5.8 8.4 %collective-permute-start = (bf16[8,128,128]{2,1,0:T(8,128)(2,1)S(1)}, bf16[8,128,128]{2,1,0:T(8,128)(2,1)S(1)}, u32[]{:S(2)}, u32[]{:S(2)}) collective-permute-start(bf16[8,128,128]{2,1,0:T(8,128)(2,1)S(1)} %bitcast.6), channel_id=1, source_target_pairs={{0,64},{64,128},{128,192},{192,256},{256,320},{320,384},{384,448},... | collective-permute-start | bytes 786440 | tf_op jit(solution)/shard_map/ppermute | solution.py:296
  6.5 10.4 %collective-permute-start.5 = (bf16[8,128,128]{2,1,0:T(8,128)(2,1)S(1)}, bf16[8,128,128]{2,1,0:T(8,128)(2,1)S(1)}, u32[]{:S(2)}, u32[]{:S(2)}) collective-permute-start(bf16[8,128,128]{2,1,0:T(8,128)(2,1)S(1)} %bitcast.7), channel_id=1, source_target_pairs={{0,32},{64,96},{128,160},{192,224},{256,288},{320,352},{384,416},{... | collective-permute-start | bytes 786440 | tf_op jit(solution)/shard_map/ppermute | solution.py:296
  10.1 6.9 %collective-permute-start.4 = (bf16[8,128,128]{2,1,0:T(8,128)(2,1)S(1)}, bf16[8,128,128]{2,1,0:T(8,128)(2,1)S(1)}, u32[]{:S(2)}, u32[]{:S(2)}) collective-permute-start(bf16[8,128,128]{2,1,0:T(8,128)(2,1)S(1)} %collective-permute-done.2.second_mid_ref), channel_id=1, source_target_pairs={{96,128},{160,192},{224,256},{288,320},{352,384},{416,448},{480,51... | collective-permute-start | bytes 786440 | tf_op jit(solution)/shard_map/ppermute | solution.py:296
  12.9 4.1 %collective-permute-start.3 = (bf16[8,128,128]{2,1,0:T(8,128)(2,1)S(1)}, bf16[8,128,128]{2,1,0:T(8,128)(2,1)S(1)}, u32[]{:S(2)}, u32[]{:S(2)}) collective-permute-start(bf16[8,128,128]{2,1,0:T(8,128)(2,1)S(1)} %collective-permute-done.2.second_mid_ref), channel_id=1, source_target_pairs={{96,64},{160,128},{224,192},{288,256},{352,320},{416,384},{480,448... | collective-permute-start | bytes 786440 | tf_op jit(solution)/shard_map/ppermute | solution.py:296
  14.2 5.6 %collective-permute-start.1 = (bf16[8,128,128]{2,1,0:T(8,128)(2,1)S(1)}, bf16[8,128,128]{2,1,0:T(8,128)(2,1)S(1)}, u32[]{:S(2)}, u32[]{:S(2)}) collective-permute-start(bf16[8,128,128]{2,1,0:T(8,128)(2,1)S(1)} %collective-permute-done.first_mid_ref), channel_id=1, source_target_pairs={{64,96},{128,160},{192,224},{256,288},{320,352},{384,416},{448,480... | collective-permute-start | bytes 786440 | tf_op jit(solution)/shard_map/ppermute | solution.py:296

commit v3 on v2

--- a/solution.py
+++ b/solution.py
@@ -242,7 +242,11 @@
         def _(half):
             attend_rows([half], 2)
 
-    @pl.when(remote_blocks >= 2)
+    @pl.when(remote_blocks == 2)
+    def _():
+        attend_rows(range(halves), 3)
+
+    @pl.when(remote_blocks > 2)
     def _():
         attend_rows(range(halves), 4)
 

time: 22.8 us -> 22.8 us (level)
  no operation moved by 1% of the time
where the time goes in v3:
time: 22.8 us; the launch traced here: 22.6 us
  starting transfers between devices  11.4 us (50%)
  waiting for transfers between devices  5.04 us (22%)
  Pallas kernels  4.2 us (18%)
  other arithmetic  1.16 us (5%)
  between operations  0.73 us (3%)
    ppermute x6, starting transfers between devices, move(): lax.ppermute(array, 'ctx', [(i, i + by) for i in starts if 0 <= i + by <...  11.4 us
    ppermute x6, waiting for transfers between devices, move(): lax.ppermute(array, 'ctx', [(i, i + by) for i in starts if 0 <= i + by <...  5.04 us
    pallas_call x1, Pallas kernels, attend(): pl.pallas_call(attend_kernel, out_shape=(jax.ShapeDtypeStruct((tokens, qu...  2.77 us
    pallas_call x1, Pallas kernels, prepare(): pl.pallas_call(prepare_kernel, out_shape=(jax.ShapeDtypeStruct((kv_heads,...  1.44 us
    transpose x1, other arithmetic, per_device(): own = jnp.stack((key_proj, value_projection)).transpose(0, 2, 1, 3)  1.16 us
  transfers between devices with their start and end apart: 6, of which 2 were waited for; matrix products, arithmetic and copies ran while one was open for 0% of the time, Pallas kernels for 6%

profile of v3, /device:TPU:65, one launch (start us, length us, event | category | flops | bytes accessed | tf_op | source)
XLA Modules:
  0.0 22.6 jit_solution(18237825067957095260)
XLA Ops:
  0.6 1.2 %maximum_bitcast_fusion = bf16[2,4,128,128]{3,1,2,0:T(4,128)(2,1)S(1)} fusion(bf16[1,128,4,128]{3,2,1,0:T(4,128)(2,1)} %bitcast.9, bf16[1,128,4,128]{3,2,1,0:T(4,128)(2,1)} %bitcast.10), kind=kLoop, calls=%fused_computation | loop fusion | flops 131072 | bytes 524288 | tf_op jit(solution)/shard_map/transpose | solution.py:295
  1.8 4.0 %collective-permute-start.2 = (bf16[8,128,128]{2,1,0:T(8,128)(2,1)S(1)}, bf16[8,128,128]{2,1,0:T(8,128)(2,1)S(1)}, u32[]{:S(2)}, u32[]{:S(2)}) collective-permute-start(bf16[8,128,128]{2,1,0:T(8,128)(2,1)S(1)} %bitcast.5), channel_id=1, source_target_pairs={{32,96},{96,160},{160,224},{224,288},{288,352},{352,416},{416,480}... | collective-permute-start | bytes 786440 | tf_op jit(solution)/shard_map/ppermute | solution.py:300
  5.8 0.7 %collective-permute-start = (bf16[8,128,128]{2,1,0:T(8,128)(2,1)S(1)}, bf16[8,128,128]{2,1,0:T(8,128)(2,1)S(1)}, u32[]{:S(2)}, u32[]{:S(2)}) collective-permute-start(bf16[8,128,128]{2,1,0:T(8,128)(2,1)S(1)} %bitcast.6), channel_id=1, source_target_pairs={{0,64},{64,128},{128,192},{192,256},{256,320},{320,384},{384,448},... | collective-permute-start | bytes 786440 | tf_op jit(solution)/shard_map/ppermute | solution.py:300
  6.5 1.3 %collective-permute-start.5 = (bf16[8,128,128]{2,1,0:T(8,128)(2,1)S(1)}, bf16[8,128,128]{2,1,0:T(8,128)(2,1)S(1)}, u32[]{:S(2)}, u32[]{:S(2)}) collective-permute-start(bf16[8,128,128]{2,1,0:T(8,128)(2,1)S(1)} %bitcast.7), channel_id=1, source_target_pairs={{0,32},{64,96},{128,160},{192,224},{256,288},{320,352},{384,416},{... | collective-permute-start | bytes 786440 | tf_op jit(solution)/shard_map/ppermute | solution.py:300
  7.8 2.2 %collective-permute-done.2.second_mid_ref = bf16[8,128,128]{2,1,0:T(8,128)(2,1)S(1)} collective-permute-done((bf16[8,128,128]{2,1,0:T(8,128)(2,1)S(1)}, bf16[8,128,128]{2,1,0:T(8,128)(2,1)S(1)}, u32[]{:S(2)}, u32[]{:S(2)}) %collective-permute-start.2) | collective-permute-done | bytes 262176 | tf_op jit(solution)/shard_map/ppermute | solution.py:300
  10.1 2.8 %collective-permute-start.4 = (bf16[8,128,128]{2,1,0:T(8,128)(2,1)S(1)}, bf16[8,128,128]{2,1,0:T(8,128)(2,1)S(1)}, u32[]{:S(2)}, u32[]{:S(2)}) collective-permute-start(bf16[8,128,128]{2,1,0:T(8,128)(2,1)S(1)} %collective-permute-done.2.second_mid_ref), channel_id=1, source_target_pairs={{96,128},{160,192},{224,256},{288,320},{352,384},{416,448},{480,51... | collective-permute-start | bytes 786440 | tf_op jit(solution)/shard_map/ppermute | solution.py:300
  12.9 1.3 %collective-permute-start.3 = (bf16[8,128,128]{2,1,0:T(8,128)(2,1)S(1)}, bf16[8,128,128]{2,1,0:T(8,128)(2,1)S(1)}, u32[]{:S(2)}, u32[]{:S(2)}) collective-permute-start(bf16[8,128,128]{2,1,0:T(8,128)(2,1)S(1)} %collective-permute-done.2.second_mid_ref), channel_id=1, source_target_pairs={{96,64},{160,128},{224,192},{288,256},{352,320},{416,384},{480,448... | collective-permute-start | bytes 786440 | tf_op jit(solution)/shard_map/ppermute | solution.py:300
  14.2 0.0 collective-permute-done.first_mid_ref
  14.2 1.3 %collective-permute-start.1 = (bf16[8,128,128]{2,1,0:T(8,128)(2,1)S(1)}, bf16[8,128,128]{2,1,0:T(8,128)(2,1)S(1)}, u32[]{:S(2)}, u32[]{:S(2)}) collective-permute-start(bf16[8,128,128]{2,1,0:T(8,128)(2,1)S(1)} %collective-permute-done.first_mid_ref), channel_id=1, source_target_pairs={{64,96},{128,160},{192,224},{256,288},{320,352},{384,416},{448,480... | collective-permute-start | bytes 786440 | tf_op jit(solution)/shard_map/ppermute | solution.py:300
  15.5 1.4 %prepare.1 = (bf16[4,1024,128]{2,1,0:T(8,128)(2,1)S(1)}, f32[4,128,8,128]{3,2,1,0:T(8,128)S(1)}, s32[8,128]{1,0:T(8,128)S(1)}) custom-call(s32[48]{0:T(128)} %all_lengths_ref.1, bf16[128,32,128]{2,1,0:T(8,128)(2,1)} %query_ref.1), custom_call_target="tpu_custom_call" | custom-call | tf_op jit(solution)/shard_map/prepare/pallas_call | solution.py:71
  17.0 0.0 collective-permute-done.5.second_near_ref
  17.0 0.0 collective-permute-done.4.first_far_ref
  17.0 0.0 collective-permute-done.3.first_near_ref
  17.0 2.8 %collective-permute-done.1.second_far_ref = bf16[8,128,128]{2,1,0:T(8,128)(2,1)S(1)} collective-permute-done((bf16[8,128,128]{2,1,0:T(8,128)(2,1)S(1)}, bf16[8,128,128]{2,1,0:T(8,128)(2,1)S(1)}, u32[]{:S(2)}, u32[]{:S(2)}) %collective-permute-start.1) | collective-permute-done | bytes 262176 | tf_op jit(solution)/shard_map/ppermute | solution.py:300
  19.8 2.8 %attend.1 = (bf16[128,32,128]{2,1,0:T(8,128)(2,1)}, f32[32,128]{1,0:T(8,128)}) custom-call(s32[8,128]{1,0:T(8,128)S(1)} %get-tuple-element.5.blocks_ref, bf16[4,1024,128]{2,1,0:T(8,128)(2,1)S(1)} %get-tuple-element.6.query_ref, f32[4,128,8,128]{3,2,1,0:T(8,128)S(1)} %get-tuple-element.7.bias_ref, bf16[8,128,128]{2,1,0:T(8,128)(2,1)S(1)} %bitcast.8, ...), custom_call_target="tpu_custom_call" | custom-call | tf_op jit(solution)/shard_map/attend/pallas_call | solution.py:269
  (1 shorter events, 0.0 us)
Async XLA Ops:
  1.8 8.2 %collective-permute-start.2 = (bf16[8,128,128]{2,1,0:T(8,128)(2,1)S(1)}, bf16[8,128,128]{2,1,0:T(8,128)(2,1)S(1)}, u32[]{:S(2)}, u32[]{:S(2)}) collective-permute-start(bf16[8,128,128]{2,1,0:T(8,128)(2,1)S(1)} %bitcast.5), channel_id=1, source_target_pairs={{32,96},{96,160},{160,224},{224,288},{288,352},{352,416},{416,480}... | collective-permute-start | bytes 786440 | tf_op jit(solution)/shard_map/ppermute | solution.py:300
  5.8 8.4 %collective-permute-start = (bf16[8,128,128]{2,1,0:T(8,128)(2,1)S(1)}, bf16[8,128,128]{2,1,0:T(8,128)(2,1)S(1)}, u32[]{:S(2)}, u32[]{:S(2)}) collective-permute-start(bf16[8,128,128]{2,1,0:T(8,128)(2,1)S(1)} %bitcast.6), channel_id=1, source_target_pairs={{0,64},{64,128},{128,192},{192,256},{256,320},{320,384},{384,448},... | collective-permute-start | bytes 786440 | tf_op jit(solution)/shard_map/ppermute | solution.py:300
  6.5 10.4 %collective-permute-start.5 = (bf16[8,128,128]{2,1,0:T(8,128)(2,1)S(1)}, bf16[8,128,128]{2,1,0:T(8,128)(2,1)S(1)}, u32[]{:S(2)}, u32[]{:S(2)}) collective-permute-start(bf16[8,128,128]{2,1,0:T(8,128)(2,1)S(1)} %bitcast.7), channel_id=1, source_target_pairs={{0,32},{64,96},{128,160},{192,224},{256,288},{320,352},{384,416},{... | collective-permute-start | bytes 786440 | tf_op jit(solution)/shard_map/ppermute | solution.py:300
  10.1 6.9 %collective-permute-start.4 = (bf16[8,128,128]{2,1,0:T(8,128)(2,1)S(1)}, bf16[8,128,128]{2,1,0:T(8,128)(2,1)S(1)}, u32[]{:S(2)}, u32[]{:S(2)}) collective-permute-start(bf16[8,128,128]{2,1,0:T(8,128)(2,1)S(1)} %collective-permute-done.2.second_mid_ref), channel_id=1, source_target_pairs={{96,128},{160,192},{224,256},{288,320},{352,384},{416,448},{480,51... | collective-permute-start | bytes 786440 | tf_op jit(solution)/shard_map/ppermute | solution.py:300
  12.9 4.1 %collective-permute-start.3 = (bf16[8,128,128]{2,1,0:T(8,128)(2,1)S(1)}, bf16[8,128,128]{2,1,0:T(8,128)(2,1)S(1)}, u32[]{:S(2)}, u32[]{:S(2)}) collective-permute-start(bf16[8,128,128]{2,1,0:T(8,128)(2,1)S(1)} %collective-permute-done.2.second_mid_ref), channel_id=1, source_target_pairs={{96,64},{160,128},{224,192},{288,256},{352,320},{416,384},{480,448... | collective-permute-start | bytes 786440 | tf_op jit(solution)/shard_map/ppermute | solution.py:300
  14.2 5.6 %collective-permute-start.1 = (bf16[8,128,128]{2,1,0:T(8,128)(2,1)S(1)}, bf16[8,128,128]{2,1,0:T(8,128)(2,1)S(1)}, u32[]{:S(2)}, u32[]{:S(2)}) collective-permute-start(bf16[8,128,128]{2,1,0:T(8,128)(2,1)S(1)} %collective-permute-done.first_mid_ref), channel_id=1, source_target_pairs={{64,96},{128,160},{192,224},{256,288},{320,352},{384,416},{448,480... | collective-permute-start | bytes 786440 | tf_op jit(solution)/shard_map/ppermute | solution.py:300

commit v4 on v2

--- a/solution.py
+++ b/solution.py
@@ -15,7 +15,7 @@
 
 
 def prepare_kernel(
-    all_lengths_ref, query_ref, grouped_ref, bias_ref, blocks_ref, lengths_ref, rows_ref, known, came
+    all_lengths_ref, query_ref, grouped_ref, bias_ref, reach_ref, lengths_ref, rows_ref, known, came
 ):
     tokens, query_heads, size = query_ref.shape
     kv_heads = grouped_ref.shape[0]
@@ -46,7 +46,9 @@
         start = jnp.where(end <= base, end, start)
         inside = jnp.where(end > base, end - base, tokens)
         rows_of_first = jnp.minimum(rows_of_first, inside)
-    blocks_ref[...] = jnp.full(blocks_ref.shape, (base - start + tokens - 1) // tokens, jnp.int32)
+    both = jnp.where(rows_of_first > half_rows, 1, 2)
+    reach = jnp.where(base - start > tokens, both, 0)
+    reach_ref[...] = jnp.full(reach_ref.shape, reach, jnp.int32)
     by_key = jnp.broadcast_to(document[:1].astype(jnp.float32), (tokens, tokens))
     by_row = by_key.T
     own_bias = jnp.where((by_key == by_row) & (lane <= row), 0.0, hidden)
@@ -92,7 +94,7 @@
 
 
 def attend_kernel(
-    blocks_ref,
+    reach_ref,
     query_ref,
     bias_ref,
     own_ref,
@@ -119,7 +121,7 @@
     scale = 1.0 / math.sqrt(size)
     shard = lax.axis_index("ctx")
     second = lax.rem(shard, 2) == 1
-    remote_blocks = blocks_ref[0, 0]
+    reach = reach_ref[0, 0]
 
     def place(block, pair_ref):
         rows = slice(block * tokens, (block + 1) * tokens)
@@ -154,11 +156,10 @@
             rows_ref.at[pair, half], out_ref.at[rows, heads], sent.at[pair, half]
         )
 
-    def attend_rows(its_halves, blocks):
-        low = 4 - blocks
+    def attend_rows(blocks_of):
         work = [
             (half, pair, 2 * pair + head, first)
-            for half in its_halves
+            for half in range(halves)
             for pair in range(pairs)
             for head in range(2)
             for first in range(0, half_rows, chunk_rows)
@@ -176,6 +177,7 @@
 
         def score(item):
             half, _, head, first = item
+            low = 4 - blocks_of[half]
             return lax.dot_general(
                 query_ref[head, pl.ds(start_of(half, first) * group, chunk), :],
                 key_ref[head, low * tokens :, :],
@@ -185,6 +187,8 @@
 
         def weigh(item, scores):
             half, _, _, first = item
+            blocks = blocks_of[half]
+            low = 4 - blocks
             parts = []
             for block in range(blocks):
                 part = scores[:, block * tokens : (block + 1) * tokens]
@@ -199,6 +203,7 @@
 
         def gather(item, top, weights):
             half, pair, head, first = item
+            low = 4 - blocks_of[half]
             total = jnp.dot(
                 weights, value_ref[head, low * tokens :, :], preferred_element_type=jnp.float32
             )
@@ -236,15 +241,17 @@
 
     totals_ref[...] = jnp.ones_like(totals_ref)
 
-    @pl.when(remote_blocks < 2)
-    def _():
-        @pl.loop(0, halves)
-        def _(half):
-            attend_rows([half], 2)
-
-    @pl.when(remote_blocks >= 2)
-    def _():
-        attend_rows(range(halves), 4)
+    @pl.when(reach == 0)
+    def _():
+        attend_rows((2, 2))
+
+    @pl.when(reach == 1)
+    def _():
+        attend_rows((4, 4))
+
+    @pl.when(reach == 2)
+    def _():
+        attend_rows((4, 2))
 
     logs_ref[...] = totals_ref[0] * scale + jnp.log(totals_ref[1])
     log_copy = pltpu.make_async_copy(logs_ref, log_ref, log_sent)
@@ -256,7 +263,7 @@
 
 
 def attend(prepared, own, earlier):
-    grouped, bias, remote_blocks = prepared
+    grouped, bias, reach = prepared
     kv_heads, tokens, size = own.shape[0] // 2, own.shape[1], own.shape[2]
     group = grouped.shape[1] // tokens
     query_heads = kv_heads * group
@@ -282,7 +289,7 @@
         ],
         compiler_params=pltpu.CompilerParams(vmem_limit_bytes=24 * 1024 * 1024),
         name="attend",
-    )(remote_blocks, grouped, bias, own, *earlier)
+    )(reach, grouped, bias, own, *earlier)
 
 
 def per_device(query_proj, key_proj, value_projection, lengths):

time: 22.8 us -> 22.7 us (level)
  the two profiles are of different devices: /device:TPU:65 before, /device:TPU:227 now
where the time goes in v4:
time: 22.7 us; the launch traced here: 22.5 us
  starting transfers between devices  12.6 us (56%)
  Pallas kernels  5.06 us (22%)
  waiting for transfers between devices  2.89 us (13%)
  other arithmetic  1.16 us (5%)
  between operations  0.73 us (3%)
    ppermute x6, starting transfers between devices, move(): lax.ppermute(array, 'ctx', [(i, i + by) for i in starts if 0 <= i + by <...  12.6 us
    pallas_call x1, Pallas kernels, attend(): pl.pallas_call(attend_kernel, out_shape=(jax.ShapeDtypeStruct((tokens, qu...  3.62 us
    ppermute x6, waiting for transfers between devices, move(): lax.ppermute(array, 'ctx', [(i, i + by) for i in starts if 0 <= i + by <...  2.89 us
    pallas_call x1, Pallas kernels, prepare(): pl.pallas_call(prepare_kernel, out_shape=(jax.ShapeDtypeStruct((kv_heads,...  1.44 us
    transpose x1, other arithmetic, per_device(): own = jnp.stack((key_proj, value_projection)).transpose(0, 2, 1, 3)  1.16 us
  transfers between devices with their start and end apart: 6, of which 2 were waited for; matrix products, arithmetic and copies ran while one was open for 0% of the time, Pallas kernels for 6%

profile of v4, /device:TPU:227, one launch (start us, length us, event | category | flops | bytes accessed | tf_op | source)
XLA Modules:
  0.0 22.5 jit_solution(4561765789391258818)
XLA Ops:
  0.6 1.2 %maximum_bitcast_fusion = bf16[2,4,128,128]{3,1,2,0:T(4,128)(2,1)S(1)} fusion(bf16[1,128,4,128]{3,2,1,0:T(4,128)(2,1)} %bitcast.9, bf16[1,128,4,128]{3,2,1,0:T(4,128)(2,1)} %bitcast.10), kind=kLoop, calls=%fused_computation | loop fusion | flops 131072 | bytes 524288 | tf_op jit(solution)/shard_map/transpose | solution.py:298
  1.8 5.2 %collective-permute-start.2 = (bf16[8,128,128]{2,1,0:T(8,128)(2,1)S(1)}, bf16[8,128,128]{2,1,0:T(8,128)(2,1)S(1)}, u32[]{:S(2)}, u32[]{:S(2)}) collective-permute-start(bf16[8,128,128]{2,1,0:T(8,128)(2,1)S(1)} %bitcast.5), channel_id=1, source_target_pairs={{32,96},{96,160},{160,224},{224,288},{288,352},{352,416},{416,480}... | collective-permute-start | bytes 786440 | tf_op jit(solution)/shard_map/ppermute | solution.py:303
  7.1 0.7 %collective-permute-start = (bf16[8,128,128]{2,1,0:T(8,128)(2,1)S(1)}, bf16[8,128,128]{2,1,0:T(8,128)(2,1)S(1)}, u32[]{:S(2)}, u32[]{:S(2)}) collective-permute-start(bf16[8,128,128]{2,1,0:T(8,128)(2,1)S(1)} %bitcast.6), channel_id=1, source_target_pairs={{0,64},{64,128},{128,192},{192,256},{256,320},{320,384},{384,448},... | collective-permute-start | bytes 786440 | tf_op jit(solution)/shard_map/ppermute | solution.py:303
  7.7 1.3 %collective-permute-start.5 = (bf16[8,128,128]{2,1,0:T(8,128)(2,1)S(1)}, bf16[8,128,128]{2,1,0:T(8,128)(2,1)S(1)}, u32[]{:S(2)}, u32[]{:S(2)}) collective-permute-start(bf16[8,128,128]{2,1,0:T(8,128)(2,1)S(1)} %bitcast.7), channel_id=1, source_target_pairs={{0,32},{64,96},{128,160},{192,224},{256,288},{320,352},{384,416},{... | collective-permute-start | bytes 786440 | tf_op jit(solution)/shard_map/ppermute | solution.py:303
  9.0 2.2 %collective-permute-done.2.second_mid_ref = bf16[8,128,128]{2,1,0:T(8,128)(2,1)S(1)} collective-permute-done((bf16[8,128,128]{2,1,0:T(8,128)(2,1)S(1)}, bf16[8,128,128]{2,1,0:T(8,128)(2,1)S(1)}, u32[]{:S(2)}, u32[]{:S(2)}) %collective-permute-start.2) | collective-permute-done | bytes 262176 | tf_op jit(solution)/shard_map/ppermute | solution.py:303
  11.3 2.8 %collective-permute-start.4 = (bf16[8,128,128]{2,1,0:T(8,128)(2,1)S(1)}, bf16[8,128,128]{2,1,0:T(8,128)(2,1)S(1)}, u32[]{:S(2)}, u32[]{:S(2)}) collective-permute-start(bf16[8,128,128]{2,1,0:T(8,128)(2,1)S(1)} %collective-permute-done.2.second_mid_ref), channel_id=1, source_target_pairs={{96,128},{160,192},{224,256},{288,320},{352,384},{416,448},{480,51... | collective-permute-start | bytes 786440 | tf_op jit(solution)/shard_map/ppermute | solution.py:303
  14.1 1.3 %collective-permute-start.3 = (bf16[8,128,128]{2,1,0:T(8,128)(2,1)S(1)}, bf16[8,128,128]{2,1,0:T(8,128)(2,1)S(1)}, u32[]{:S(2)}, u32[]{:S(2)}) collective-permute-start(bf16[8,128,128]{2,1,0:T(8,128)(2,1)S(1)} %collective-permute-done.2.second_mid_ref), channel_id=1, source_target_pairs={{96,64},{160,128},{224,192},{288,256},{352,320},{416,384},{480,448... | collective-permute-start | bytes 786440 | tf_op jit(solution)/shard_map/ppermute | solution.py:303
  15.4 0.0 collective-permute-done.first_mid_ref
  15.4 1.3 %collective-permute-start.1 = (bf16[8,128,128]{2,1,0:T(8,128)(2,1)S(1)}, bf16[8,128,128]{2,1,0:T(8,128)(2,1)S(1)}, u32[]{:S(2)}, u32[]{:S(2)}) collective-permute-start(bf16[8,128,128]{2,1,0:T(8,128)(2,1)S(1)} %collective-permute-done.first_mid_ref), channel_id=1, source_target_pairs={{64,96},{128,160},{192,224},{256,288},{320,352},{384,416},{448,480... | collective-permute-start | bytes 786440 | tf_op jit(solution)/shard_map/ppermute | solution.py:303
  16.7 1.4 %prepare.1 = (bf16[4,1024,128]{2,1,0:T(8,128)(2,1)S(1)}, f32[4,128,8,128]{3,2,1,0:T(8,128)S(1)}, s32[8,128]{1,0:T(8,128)S(1)}) custom-call(s32[48]{0:T(128)} %all_lengths_ref.1, bf16[128,32,128]{2,1,0:T(8,128)(2,1)} %query_ref.1), custom_call_target="tpu_custom_call" | custom-call | tf_op jit(solution)/shard_map/prepare/pallas_call | solution.py:73
  18.2 0.0 collective-permute-done.5.second_near_ref
  18.2 0.0 collective-permute-done.4.first_far_ref
  18.2 0.0 collective-permute-done.3.first_near_ref
  18.2 0.7 %collective-permute-done.1.second_far_ref = bf16[8,128,128]{2,1,0:T(8,128)(2,1)S(1)} collective-permute-done((bf16[8,128,128]{2,1,0:T(8,128)(2,1)S(1)}, bf16[8,128,128]{2,1,0:T(8,128)(2,1)S(1)}, u32[]{:S(2)}, u32[]{:S(2)}) %collective-permute-start.1) | collective-permute-done | bytes 262176 | tf_op jit(solution)/shard_map/ppermute | solution.py:303
  18.9 3.6 %attend.1 = (bf16[128,32,128]{2,1,0:T(8,128)(2,1)}, f32[32,128]{1,0:T(8,128)}) custom-call(s32[8,128]{1,0:T(8,128)S(1)} %get-tuple-element.5.reach_ref, bf16[4,1024,128]{2,1,0:T(8,128)(2,1)S(1)} %get-tuple-element.6.query_ref, f32[4,128,8,128]{3,2,1,0:T(8,128)S(1)} %get-tuple-element.7.bias_ref, bf16[8,128,128]{2,1,0:T(8,128)(2,1)S(1)} %bitcast.8, ...), custom_call_target="tpu_custom_call" | custom-call | tf_op jit(solution)/shard_map/attend/pallas_call | solution.py:272
  (1 shorter events, 0.0 us)
Async XLA Ops:
  1.8 9.4 %collective-permute-start.2 = (bf16[8,128,128]{2,1,0:T(8,128)(2,1)S(1)}, bf16[8,128,128]{2,1,0:T(8,128)(2,1)S(1)}, u32[]{:S(2)}, u32[]{:S(2)}) collective-permute-start(bf16[8,128,128]{2,1,0:T(8,128)(2,1)S(1)} %bitcast.5), channel_id=1, source_target_pairs={{32,96},{96,160},{160,224},{224,288},{288,352},{352,416},{416,480}... | collective-permute-start | bytes 786440 | tf_op jit(solution)/shard_map/ppermute | solution.py:303
  7.1 8.4 %collective-permute-start = (bf16[8,128,128]{2,1,0:T(8,128)(2,1)S(1)}, bf16[8,128,128]{2,1,0:T(8,128)(2,1)S(1)}, u32[]{:S(2)}, u32[]{:S(2)}) collective-permute-start(bf16[8,128,128]{2,1,0:T(8,128)(2,1)S(1)} %bitcast.6), channel_id=1, source_target_pairs={{0,64},{64,128},{128,192},{192,256},{256,320},{320,384},{384,448},... | collective-permute-start | bytes 786440 | tf_op jit(solution)/shard_map/ppermute | solution.py:303
  7.7 10.4 %collective-permute-start.5 = (bf16[8,128,128]{2,1,0:T(8,128)(2,1)S(1)}, bf16[8,128,128]{2,1,0:T(8,128)(2,1)S(1)}, u32[]{:S(2)}, u32[]{:S(2)}) collective-permute-start(bf16[8,128,128]{2,1,0:T(8,128)(2,1)S(1)} %bitcast.7), channel_id=1, source_target_pairs={{0,32},{64,96},{128,160},{192,224},{256,288},{320,352},{384,416},{... | collective-permute-start | bytes 786440 | tf_op jit(solution)/shard_map/ppermute | solution.py:303
  11.3 6.9 %collective-permute-start.4 = (bf16[8,128,128]{2,1,0:T(8,128)(2,1)S(1)}, bf16[8,128,128]{2,1,0:T(8,128)(2,1)S(1)}, u32[]{:S(2)}, u32[]{:S(2)}) collective-permute-start(bf16[8,128,128]{2,1,0:T(8,128)(2,1)S(1)} %collective-permute-done.2.second_mid_ref), channel_id=1, source_target_pairs={{96,128},{160,192},{224,256},{288,320},{352,384},{416,448},{480,51... | collective-permute-start | bytes 786440 | tf_op jit(solution)/shard_map/ppermute | solution.py:303
  14.1 4.1 %collective-permute-start.3 = (bf16[8,128,128]{2,1,0:T(8,128)(2,1)S(1)}, bf16[8,128,128]{2,1,0:T(8,128)(2,1)S(1)}, u32[]{:S(2)}, u32[]{:S(2)}) collective-permute-start(bf16[8,128,128]{2,1,0:T(8,128)(2,1)S(1)} %collective-permute-done.2.second_mid_ref), channel_id=1, source_target_pairs={{96,64},{160,128},{224,192},{288,256},{352,320},{416,384},{480,448... | collective-permute-start | bytes 786440 | tf_op jit(solution)/shard_map/ppermute | solution.py:303
  15.4 3.4 %collective-permute-start.1 = (bf16[8,128,128]{2,1,0:T(8,128)(2,1)S(1)}, bf16[8,128,128]{2,1,0:T(8,128)(2,1)S(1)}, u32[]{:S(2)}, u32[]{:S(2)}) collective-permute-start(bf16[8,128,128]{2,1,0:T(8,128)(2,1)S(1)} %collective-permute-done.first_mid_ref), channel_id=1, source_target_pairs={{64,96},{128,160},{192,224},{256,288},{320,352},{384,416},{448,480... | collective-permute-start | bytes 786440 | tf_op jit(solution)/shard_map/ppermute | solution.py:303
